TPU v7x, 32 devices: a whole 2x2x4 slice. The times are simulated.
32 devices in a mesh: ctx: 4 (over y, x), exp: 4 (over z), tp: 2 (over core).
Axes of the slice: x: 2, y: 2, z: 4, core: 2. Of those that a mesh axis runs over, the one named last changes fastest.
Arguments:
- queries: bfloat16 [512, 36864], P('ctx', ('exp', 'tp')), may hold values from -90 to 90
- latent_keys: bfloat16 [512, 576], P('ctx'), may hold values from -6 to 6
- block_order: int32 [4], replicated, may hold values from 0 to 3, each once
- moe_input: bfloat16 [512, 3584], P(('ctx', 'exp')), may hold values from -6 to 6
- routes: int32 [512, 2], P(('ctx', 'exp')), may hold values from 0 to 3, all different within a row; in each aligned block of 32 rows (0 to 31, 32 to 63, ...) at most 32 rows name the same one
- gate_weights: float32 [512, 2], P(('ctx', 'exp')), may hold values from 0.2 to 1
- w_gate: bfloat16 [4, 3584, 1024], P('exp', 'ctx', 'tp'), may hold values from -0.09375 to 0.09375
- w_up: bfloat16 [4, 3584, 1024], P('exp', 'ctx', 'tp'), may hold values from -0.09375 to 0.09375
- w_down: bfloat16 [4, 1024, 3584], P('exp', 'ctx', 'tp'), may hold values from -0.1875 to 0.1875
Outputs:
- context: bfloat16 [512, 32768], P('ctx', ('exp', 'tp'))
- moe_out: bfloat16 [512, 3584], P(('ctx', 'exp'), 'tp')
Inputs may be any that keep to these rules, and one draw needn't show every extreme that they name: `routes`: within the 32 rows of one device no expert is named by more than 32 rows, and some expert reaches 32. `block_order`: each block index appears once.
All inputs are finite; a program needn't handle non-finite values.
Results may differ from a plain program's by a relative error of at most 0.0065.
Values may be sent and summed in bfloat16 or wider, within the bound.
A program may use at most 64 MiB of HBM per device.

v0:
```python
import jax
import jax.numpy as jnp
from jax import lax
from jax.sharding import PartitionSpec as P

LATENT = 512
ROPE = 64


softmax_scale = 0.07216878364870323
very_negative = -1e30


def passed_along(block, axis, distance):
    devices = range(lax.axis_size(axis))
    route = [((i - distance) % len(devices), i) for i in devices]
    return lax.ppermute(block, axis, route)


def slot_table(route_rows, experts, capacity):
    flat_ids = route_rows.reshape(-1)
    one_hot = (flat_ids[:, None] == jnp.arange(experts, dtype=jnp.int32)[None, :]).astype(jnp.int32)
    earlier = jnp.cumsum(one_hot, axis=0) - one_hot
    ranking = jnp.sum(earlier * one_hot, axis=1)
    return flat_ids * capacity + ranking


def body(queries, latent_keys, block_order, moe_input, routes, gate_weights, w_gate, w_up, w_down):
    full_gate, full_up, full_down = (
        lax.all_gather(w_gate, "ctx", axis=1, tiled=True),
        lax.all_gather(w_up, "ctx", axis=1, tiled=True),
        lax.all_gather(w_down, "ctx", axis=1, tiled=True),
    )
    full_width = LATENT + ROPE
    block_len = queries.shape[0]
    heads_here = queries.shape[1] // full_width
    per_head = queries.reshape(block_len, heads_here, full_width)
    cycle_size = lax.axis_size("ctx")
    position = lax.axis_index("ctx")
    offsets = jnp.arange(block_len, dtype=jnp.int32)
    own_block = block_order[position]
    own_pos = own_block * block_len + offsets

    def attend(running, key_block, source):
        source_block = block_order[source]
        top_old, total_old, summed_old = running
        key_pos = source_block * block_len + offsets
        visible = (key_pos[None, :] <= own_pos[:, None]) & True
        scores = (
            jnp.einsum("thc,uc->thu", per_head, key_block, preferred_element_type=jnp.float32)
            * softmax_scale
        )
        masked = jnp.where(visible[:, None, :], scores, very_negative)
        top_new = jnp.maximum(top_old, jnp.max(masked, axis=-1))
        weights = jnp.where(visible[:, None, :], jnp.exp(masked - top_new[:, :, None]), 0.0)
        factor = jnp.exp(top_old - top_new)
        total_new = total_old * factor + jnp.sum(weights, axis=-1)
        summed_new = summed_old * factor[:, :, None] + jnp.einsum(
            "thu,uc->thc",
            weights.astype(jnp.bfloat16),
            key_block[:, :LATENT],
            preferred_element_type=jnp.float32,
        )
        return (top_new, total_new, summed_new)

    initial = (
        jnp.full((block_len, heads_here), very_negative, jnp.float32),
        jnp.zeros((block_len, heads_here), jnp.float32),
        jnp.zeros((block_len, heads_here, LATENT), jnp.float32),
    )
    running = attend(initial, latent_keys, position)

    def step_forward(step_index, carried):
        state_now, ahead_keys = carried
        ahead_keys = passed_along(ahead_keys, "ctx", 1)
        state_now = attend(state_now, ahead_keys, (position - step_index) % cycle_size)
        return (state_now, ahead_keys)

    finished = lax.fori_loop(1, cycle_size, step_forward, (running, latent_keys))
    top_score, row_total, summed = finished[0]
    context = (
        (summed / row_total[:, :, None])
        .astype(jnp.bfloat16)
        .reshape(block_len, heads_here * LATENT)
    )
    tokens_here = moe_input.shape[0]
    top_count = routes.shape[1]
    owners = lax.axis_size("exp")
    experts = w_gate.shape[0] * owners
    capacity = min(tokens_here, 2 * tokens_here * top_count // experts)
    model_width = moe_input.shape[1]
    half_width = w_down.shape[2]
    slot_index = slot_table(routes, experts, capacity)
    outgoing = (
        jnp.zeros((experts * capacity, model_width), jnp.bfloat16)
        .at[slot_index]
        .set(jnp.repeat(moe_input, top_count, axis=0))
    )
    outgoing = outgoing.reshape(owners, capacity, model_width)
    arrived = lax.all_to_all(outgoing, "exp", split_axis=0, concat_axis=0, tiled=True)
    flat_rows = arrived.reshape(-1, model_width)
    gate_proj = jnp.dot(flat_rows, full_gate[0], preferred_element_type=jnp.float32)
    upward = jnp.dot(flat_rows, full_up[0], preferred_element_type=jnp.float32)
    hidden = (jax.nn.silu(gate_proj) * upward).astype(jnp.bfloat16)
    hidden_all = lax.all_gather(hidden, "tp", axis=1, tiled=True)
    produced_rows = jnp.dot(hidden_all, full_down[0], preferred_element_type=jnp.float32).astype(
        jnp.bfloat16
    )
    produced = produced_rows.reshape(arrived.shape[0], arrived.shape[1], half_width)
    returned = lax.all_to_all(produced, "exp", split_axis=0, concat_axis=0, tiled=True)
    picked = (
        returned.reshape(-1, half_width)[slot_index]
        .astype(jnp.float32)
        .reshape(tokens_here, top_count, half_width)
    )
    moe_out = jnp.sum(picked * gate_weights[:, :, None], axis=1).astype(jnp.bfloat16)
    return (context, moe_out)


def solution(mesh):
    in_specs = (
        P("ctx", ("exp", "tp")),
        P("ctx", None),
        P(),
        P(("ctx", "exp"), None),
        P(("ctx", "exp"), None),
        P(("ctx", "exp"), None),
        P("exp", "ctx", "tp"),
        P("exp", "ctx", "tp"),
        P("exp", "ctx", "tp"),
    )
    out_specs = (P("ctx", ("exp", "tp")), P(("ctx", "exp"), "tp"))
    return jax.shard_map(body, mesh=mesh, in_specs=in_specs, out_specs=out_specs, check_vma=False)
```

profile of v0, /device:TPU:0, one launch (start us, length us, event | category | flops | bytes accessed | tf_op | source)
XLA Modules:
  0.0 206.5 jit_solution(17052133801608930887)
XLA Ops:
  7.2 0.9 copy.51
  8.2 0.7 all-gather.6.cloned.1.call-update
  9.0 0.7 all-gather.8.cloned.1.call-update
  9.8 0.1 eq.23
  10.0 0.1 mul.114
  10.1 0.2 broadcast_in_dim.106
  10.3 0.2 reshape.157
  10.6 0.1 reduce_window_sum.11
  10.7 0.2 select_reduce_fusion
  10.9 2.2 %scatter_custom_fusion = bf16[128,3584]{1,0:T(8,128)(2,1)} fusion(s32[64]{0:T(128)S(1)} %fusion.42, bf16[64,3584]{1,0:T(8,128)(2,1)S(1)} %reshape.157, bf16[]{:T(256)} %constant.127.clone.1), kind=kCustom, calls=%fused_computation.37 | custom fusion | bytes 917506 | tf_op jit(solution)/shard_map/scatter | solution.py:97
  13.1 6.4 %all-to-all-start = ((bf16[4,32,3584]{2,1,0:T(8,128)(2,1)}), bf16[4,32,3584]{2,1,0:T(8,128)(2,1)S(1)}, u32[]{:S(2)}, u32[]{:S(2)}) async-start(bf16[4,32,3584]{2,1,0:T(8,128)(2,1)} %bitcast.6), calls=%async_computation | async-start | bytes 1835008 | tf_op jit(solution)/shard_map/all_to_all | solution.py:100
  19.6 1.4 copy.22
  21.0 0.7 dynamic_slice.14
  22.4 1.7 fusion.46
  24.1 0.1 fusion.33
  24.3 0.5 convolution_add_fusion
  24.8 17.7 %all-to-all-done = bf16[4,32,3584]{2,1,0:T(8,128)(2,1)S(1)} async-done(((bf16[4,32,3584]{2,1,0:T(8,128)(2,1)}), bf16[4,32,3584]{2,1,0:T(8,128)(2,1)S(1)}, u32[]{:S(2)}, u32[]{:S(2)}) %all-to-all-start) | async-done | bytes 917536 | tf_op jit(solution)/shard_map/all_to_all | solution.py:100
  42.5 18.4 %all-gather.4.cloned.1.call-done = bf16[1,3584,512]{2,1,0:T(8,128)(2,1)} async-done(((bf16[1,896,512]{2,1,0:T(8,128)(2,1)}), bf16[1,3584,512]{2,1,0:T(8,128)(2,1)}) %all-gather.4.cloned.1.call-update) | async-done | bytes 3670032 | tf_op jit(solution)/shard_map/all_gather | solution.py:30
  60.9 2.7 %fusion.17 = f32[128,512]{1,0:T(8,128)S(1)} fusion(bf16[128,3584]{1,0:T(8,128)(2,1)S(1)} %bitcast.62, bf16[1,3584,512]{2,1,0:T(8,128)(2,1)} %all-gather.4.cloned.1.call-done), kind=kOutput, calls=%fused_computation.25 | convolution fusion | flops 469762048 | bytes 4849664 | tf_op jit(solution)/shard_map/dot_general | solution.py:102
  63.6 47.5 %all-gather.6.cloned.1.call-done = bf16[1,3584,512]{2,1,0:T(8,128)(2,1)} async-done(((bf16[1,896,512]{2,1,0:T(8,128)(2,1)}), bf16[1,3584,512]{2,1,0:T(8,128)(2,1)}) %all-gather.6.cloned.1.call-update) | async-done | bytes 3670032 | tf_op jit(solution)/shard_map/all_gather | solution.py:31
  111.2 2.7 %fusion.26 = bf16[128,512]{1,0:T(8,128)(2,1)S(1)} fusion(bf16[128,3584]{1,0:T(8,128)(2,1)S(1)} %bitcast.63, bf16[1,3584,512]{2,1,0:T(8,128)(2,1)} %all-gather.6.cloned.1.call-done, f32[128,512]{1,0:T(8,128)S(1)} %fusion.17), kind=kOutput, calls=%fused_computation.33 | convolution fusion | flops 470155264 | bytes 4980736 | tf_op jit(solution)/shard_map/dot_general | solution.py:103
  113.9 2.0 all_gather.14
  115.8 45.5 %all-gather.8.cloned.1.call-done = bf16[1,1024,1792]{2,1,0:T(8,128)(2,1)} async-done(((bf16[1,256,1792]{2,1,0:T(8,128)(2,1)}), bf16[1,1024,1792]{2,1,0:T(8,128)(2,1)}) %all-gather.8.cloned.1.call-update) | async-done | bytes 3670032 | tf_op jit(solution)/shard_map/all_gather | solution.py:32
  161.4 3.5 %fusion.19 = bf16[128,1792]{1,0:T(8,128)(2,1)} fusion(bf16[128,1024]{1,0:T(8,128)(2,1)S(1)} %all_gather.14, bf16[1,1024,1792]{2,1,0:T(8,128)(2,1)} %all-gather.8.cloned.1.call-done), kind=kOutput, calls=%fused_computation.27 | convolution fusion | flops 469991424 | bytes 4390912 | tf_op jit(solution)/shard_map/dot_general | solution.py:106
  164.9 4.6 %all-to-all-start.1 = ((bf16[4,32,1792]{2,1,0:T(8,128)(2,1)}), bf16[4,32,1792]{2,1,0:T(8,128)(2,1)S(1)}, u32[]{:S(2)}, u32[]{:S(2)}) async-start(bf16[4,32,1792]{2,1,0:T(8,128)(2,1)} %bitcast.11), calls=%async_computation.1 | async-start | bytes 917504 | tf_op jit(solution)/shard_map/all_to_all | solution.py:110
  169.5 26.8 %while.22 = (s32[]{:T(128)}, f32[128,8]{0,1:T(8,128)S(1)}, f32[128,8]{0,1:T(8,128)S(1)}, f32[128,8,512]{2,0,1:T(8,128)S(1)}, bf16[128,576]{0,1:T(8,128)(2,1)S(1)...) while((s32[]{:T(128)}, f32[128,8]{0,1:T(8,128)S(1)}, ...), condition=%wide.region_5.6_spmd.clone, body=%wide.region_2.5_spmd.clone.sunk | while | flops 287459584 | bytes 8243560 | solution.py:79
  169.5 1.5 collective-permute-start
  170.9 0.6 dynamic_slice.17
  172.3 3.4 %collective-permute-done = bf16[128,576]{0,1:T(8,128)(2,1)S(1)} collective-permute-done((bf16[128,576]{0,1:T(8,128)(2,1)S(1)}, bf16[128,576]{0,1:T(8,128)(2,1)S(1)}, u32[]{:S(2)}, u32[]{:S(2)}) %collective-permute-start) | collective-permute-done | bytes 147488 | tf_op jit(solution)/shard_map/while/body/eval_jaxpr/ppermute | solution.py:17
  175.7 1.7 fusion.58
  177.4 0.1 fusion.59
  177.6 0.9 multiply_add_fusion.5
  178.5 0.6 collective-permute-start
  179.1 0.6 dynamic_slice.17
  180.4 4.1 %collective-permute-done = bf16[128,576]{0,1:T(8,128)(2,1)S(1)} collective-permute-done((bf16[128,576]{0,1:T(8,128)(2,1)S(1)}, bf16[128,576]{0,1:T(8,128)(2,1)S(1)}, u32[]{:S(2)}, u32[]{:S(2)}) %collective-permute-start) | collective-permute-done | bytes 147488 | tf_op jit(solution)/shard_map/while/body/eval_jaxpr/ppermute | solution.py:17
  184.6 1.7 fusion.58
  186.3 0.1 fusion.59
  186.5 0.9 multiply_add_fusion.5
  187.5 0.6 dynamic_slice.17
  188.8 4.7 %collective-permute-done = bf16[128,576]{0,1:T(8,128)(2,1)S(1)} collective-permute-done((bf16[128,576]{0,1:T(8,128)(2,1)S(1)}, bf16[128,576]{0,1:T(8,128)(2,1)S(1)}, u32[]{:S(2)}, u32[]{:S(2)}) %collective-permute-start) | collective-permute-done | bytes 147488 | tf_op jit(solution)/shard_map/while/body/eval_jaxpr/ppermute | solution.py:17
  193.5 1.7 fusion.58
  195.2 0.1 fusion.59
  195.3 0.9 multiply_add_fusion.5
  196.3 0.2 fusion.29
  196.5 1.1 copy.34
  197.7 0.7 gather_fusion
  198.4 0.2 reshape.144
  198.7 1.3 multiply_reduce_fusion
  (45 shorter events, 1.0 us)
Async XLA Ops:
  7.2 2.9 %copy-start.1 = (bf16[32,3584]{1,0:T(8,128)(2,1)S(1)}, bf16[32,3584]{1,0:T(8,128)(2,1)}, u32[]{:S(2)}) copy-start(bf16[32,3584]{1,0:T(8,128)(2,1)} %param.14) | copy-start | bytes 688132
  7.2 2.5 %copy-start.2 = (s32[32,2]{0,1:T(2,128)S(1)}, s32[32,2]{0,1:T(2,128)}, u32[]{:S(2)}) copy-start(s32[32,2]{0,1:T(2,128)} %param.15) | copy-start | bytes 772
  7.2 53.8 %all-gather.4.cloned.1.call-start = ((), (), s32[]{:S(2)}) async-start(), calls=%async_computation.2 | async-start | bytes 4587520 | tf_op jit(solution)/shard_map/all_gather | solution.py:30
  8.2 103.0 %all-gather.6.cloned.1.call-start = ((), (), s32[]{:S(2)}) async-start(), calls=%async_computation.3 | async-start | bytes 4587520 | tf_op jit(solution)/shard_map/all_gather | solution.py:31
  8.9 152.5 %all-gather.8.cloned.1.call-start = ((), (), s32[]{:S(2)}) async-start(), calls=%async_computation.4 | async-start | bytes 4587520 | tf_op jit(solution)/shard_map/all_gather | solution.py:32
  10.1 9.5 %copy-start = (bf16[128,4608]{1,0:T(8,128)(2,1)S(1)}, bf16[128,4608]{1,0:T(8,128)(2,1)}, u32[]{:S(2)}) copy-start(bf16[128,4608]{1,0:T(8,128)(2,1)} %param.11) | copy-start | bytes 3538948
  13.1 7.8 %copy-start.4 = (s32[4]{0:T(128)S(1)}, s32[4]{0:T(128)}, u32[]{:S(2)}) copy-start(s32[4]{0:T(128)} %param.13) | copy-start | bytes 52
  13.1 29.4 %all-to-all-start = ((bf16[4,32,3584]{2,1,0:T(8,128)(2,1)}), bf16[4,32,3584]{2,1,0:T(8,128)(2,1)S(1)}, u32[]{:S(2)}, u32[]{:S(2)}) async-start(bf16[4,32,3584]{2,1,0:T(8,128)(2,1)} %bitcast.6), calls=%async_computation | async-start | bytes 1835008 | tf_op jit(solution)/shard_map/all_to_all | solution.py:100
  164.9 32.8 %all-to-all-start.1 = ((bf16[4,32,1792]{2,1,0:T(8,128)(2,1)}), bf16[4,32,1792]{2,1,0:T(8,128)(2,1)S(1)}, u32[]{:S(2)}, u32[]{:S(2)}) async-start(bf16[4,32,1792]{2,1,0:T(8,128)(2,1)} %bitcast.11), calls=%async_computation.1 | async-start | bytes 917504 | tf_op jit(solution)/shard_map/all_to_all | solution.py:110
  169.5 6.2 %collective-permute-start = (bf16[128,576]{0,1:T(8,128)(2,1)S(1)}, bf16[128,576]{0,1:T(8,128)(2,1)S(1)}, u32[]{:S(2)}, u32[]{:S(2)}) collective-permute-start(bf16[128,576]{0,1:T(8,128)(2,1)S(1)} %get-tuple-element.383), channel_id=1, source_target_pairs={{24,0},{0,8},{8,16},{16,24},{25,1},{1,9},{9,17},{17,25},{26,2},{2,... | collective-permute-start | bytes 442376 | tf_op jit(solution)/shard_map/while/body/eval_jaxpr/ppermute | solution.py:17
  178.5 6.1 %collective-permute-start = (bf16[128,576]{0,1:T(8,128)(2,1)S(1)}, bf16[128,576]{0,1:T(8,128)(2,1)S(1)}, u32[]{:S(2)}, u32[]{:S(2)}) collective-permute-start(bf16[128,576]{0,1:T(8,128)(2,1)S(1)} %get-tuple-element.383), channel_id=1, source_target_pairs={{24,0},{0,8},{8,16},{16,24},{25,1},{1,9},{9,17},{17,25},{26,2},{2,... | collective-permute-start | bytes 442376 | tf_op jit(solution)/shard_map/while/body/eval_jaxpr/ppermute | solution.py:17
  187.4 6.1 %collective-permute-start = (bf16[128,576]{0,1:T(8,128)(2,1)S(1)}, bf16[128,576]{0,1:T(8,128)(2,1)S(1)}, u32[]{:S(2)}, u32[]{:S(2)}) collective-permute-start(bf16[128,576]{0,1:T(8,128)(2,1)S(1)} %get-tuple-element.383), channel_id=1, source_target_pairs={{24,0},{0,8},{8,16},{16,24},{25,1},{1,9},{9,17},{17,25},{26,2},{2,... | collective-permute-start | bytes 442376 | tf_op jit(solution)/shard_map/while/body/eval_jaxpr/ppermute | solution.py:17
  196.3 1.3 copy-start.3
Sparse Core Ops, SparseCore 0:
  9.9 51.0 all-gather.3
  62.8 48.3 all-gather.5
  113.0 48.3 all-gather.7
where the time goes:
time: 207 us; the launch traced here: 206 us
  waiting for transfers between devices  143 us (69%)
  matrix products  18.8 us (9%)
  between operations  14.6 us (7%)
  starting transfers between devices  13.3 us (6%)
  local copies, waits for them, and re-layouts  9.94 us (5%)
  other arithmetic  2.71 us (1%)
  loops' own time  2.21 us (1%)
    all_gather x1, waiting for transfers between devices, body(): lax.all_gather(w_up, 'ctx', axis=1, tiled=True)  47.5 us
    all_gather x1, waiting for transfers between devices, body(): lax.all_gather(w_down, 'ctx', axis=1, tiled=True)  45.5 us
    all_gather x1, waiting for transfers between devices, body(): lax.all_gather(w_gate, 'ctx', axis=1, tiled=True)  18.4 us
    all_to_all x1, waiting for transfers between devices, body(): lax.all_to_all(outgoing, 'exp', split_axis=0, concat_axis=0, tiled=True)  17.7 us
    ppermute x3, waiting for transfers between devices, passed_along(): return lax.ppermute(block, axis, route)  12.2 us
    dot_general x4, matrix products, attend(): jnp.einsum('thc,uc->thu', per_head, key_block, preferred_element_type=jnp...  6.81 us
    all_to_all x1, starting transfers between devices, body(): lax.all_to_all(outgoing, 'exp', split_axis=0, concat_axis=0, tiled=True)  6.45 us
    all_to_all x1, starting transfers between devices, body(): lax.all_to_all(produced, 'exp', split_axis=0, concat_axis=0, tiled=True)  4.6 us
  transfers between devices with their start and end apart: 8, of which 7 were waited for; matrix products, arithmetic and copies ran while one was open for 12% of the time, Pallas kernels for 0%

commit v1 on v0

--- a/solution.py
+++ b/solution.py
@@ -1,14 +1,320 @@
+import functools
+
 import jax
 import jax.numpy as jnp
 from jax import lax
+from jax.experimental import pallas as pl
+from jax.experimental.pallas import tpu as pltpu
 from jax.sharding import PartitionSpec as P
 
 LATENT = 512
 ROPE = 64
-
+LANES = 128
+MESH = pl.DeviceIdType.MESH
 
 softmax_scale = 0.07216878364870323
 very_negative = -1e30
+
+
+def kernel(
+    n_ctx, n_exp,
+    q_hbm, k_ref, order_ref, x_ref, routes_ref, gates_ref, wg_hbm, wu_hbm, wd_hbm,
+    context_ref, moe_ref,
+    q_ref, wg_ref, wu_ref, wd_ref,
+    staged, rows, keys, gu_out, gu_in, hidden, dn_out, dn_in, z_out, z_in, home,
+    load_sem,
+    xs_s, xs_r, xz_s, xz_r, xc_s, xc_r, k_s, k_r, kc_s, kc_r,
+    gu_s, gu_r, h_s, h_r, dn_s, dn_r, zz_s, zz_r,
+):
+    c, e, t = lax.axis_index("ctx"), lax.axis_index("exp"), lax.axis_index("tp")
+    other = 1 - t
+    width = wg_ref.shape[0]
+    slice_width = wd_ref.shape[0]
+    slices = wg_ref.shape[1] // slice_width
+    tokens = x_ref.shape[0]
+    half = tokens // 2
+    block = k_ref.shape[0]
+    chunk = n_ctx * tokens
+    full_width = LATENT + ROPE
+    heads = q_ref.shape[1] // full_width
+
+    def ctx_at(step):
+        return lax.rem(c + step, n_ctx)
+
+    def exp_at(step):
+        return lax.rem(e + step, n_exp)
+
+    loads = [
+        pltpu.make_async_copy(src, dst, load_sem.at[i])
+        for i, (src, dst) in enumerate(
+            ((wg_hbm, wg_ref), (wu_hbm, wu_ref), (q_hbm, q_ref), (wd_hbm, wd_ref))
+        )
+    ]
+    for load in loads:
+        load.start()
+
+    barrier = pltpu.get_barrier_semaphore()
+    for step in range(1, n_ctx):
+        pl.semaphore_signal(barrier, inc=1, device_id={"ctx": ctx_at(step)}, device_id_type=MESH)
+    for step in range(1, n_exp):
+        pl.semaphore_signal(barrier, inc=1, device_id={"exp": exp_at(step)}, device_id_type=MESH)
+    pl.semaphore_signal(barrier, inc=1, device_id={"tp": other}, device_id_type=MESH)
+
+    lane = lax.broadcasted_iota(jnp.int32, (tokens, LANES), 1)
+    expert_lane = lax.rem(lane, n_exp)
+    dense = jnp.zeros((tokens, LANES), jnp.float32)
+    for j in range(routes_ref.shape[1]):
+        dense += jnp.where(routes_ref[:, j : j + 1] == expert_lane, gates_ref[:, j : j + 1], 0.0)
+    high = dense.astype(jnp.bfloat16).astype(jnp.float32)
+    packed = jnp.where(
+        lane < n_exp, high, jnp.where(lane < 2 * n_exp, dense - high, 0.0)
+    ).astype(jnp.bfloat16)
+    for d in range(n_ctx):
+        for part in range(2):
+            span = slice(part * half, (part + 1) * half)
+            staged[d, part, :, :width] = x_ref[span, d * width : (d + 1) * width]
+            staged[d, part, :, width:] = packed[span, :]
+    rows[e, c, t] = staged[c, t]
+    keys[c, t] = k_ref[pl.ds(pl.multiple_of(t * (block // 2), block // 2), block // 2), :]
+
+    pl.semaphore_wait(barrier, n_ctx + n_exp - 1)
+
+    sends = []
+
+    def send(src, dst, s_sem, r_sem, where):
+        copy = pltpu.make_async_remote_copy(
+            src_ref=src, dst_ref=dst, send_sem=s_sem, recv_sem=r_sem,
+            device_id=where, device_id_type=MESH,
+        )
+        copy.start()
+        return copy
+
+    def arrived(dst, s_sem, r_sem, where):
+        pltpu.make_async_remote_copy(
+            src_ref=dst, dst_ref=dst, send_sem=s_sem, recv_sem=r_sem,
+            device_id=where, device_id_type=MESH,
+        ).wait_recv()
+
+    core = {"tp": other}
+    for step in range(1, n_ctx):
+        d = ctx_at(step)
+        sends.append(send(staged.at[d, t], rows.at[e, c, t], xs_s.at[step], xs_r.at[c], {"ctx": d}))
+    for step in range(1, n_ctx):
+        d = ctx_at(step)
+        sends.append(send(keys.at[c, t], keys.at[c, t], k_s.at[step], k_r.at[c], {"ctx": d}))
+    for step in range(1, n_ctx):
+        d = ctx_at(step)
+        arrived(rows.at[e, d, t], xs_s.at[step], xs_r.at[d], {"ctx": d})
+    for step in range(1, n_exp):
+        d = exp_at(step)
+        sends.append(send(rows.at[e, :, t], rows.at[e, :, t], xz_s.at[step], xz_r.at[e], {"exp": d}))
+
+    def share_chunk(i):
+        source = exp_at(i)
+        if i:
+            arrived(rows.at[source, :, t], xz_s.at[i], xz_r.at[source], {"exp": source})
+        sends.append(
+            send(rows.at[source, :, t], rows.at[source, :, t], xc_s.at[i], xc_r.at[i], core)
+        )
+
+    def project(i):
+        source = exp_at(i)
+        arrived(rows.at[source, :, other], xc_s.at[i], xc_r.at[i], core)
+        x = rows[source].reshape(chunk, width + LANES)[:, :width]
+        for s in range(slices):
+            columns = slice(s * slice_width, (s + 1) * slice_width)
+            for at, weight in ((0, wg_ref), (slice_width, wu_ref)):
+                gu_out[i, s, :, at : at + slice_width] = jnp.dot(
+                    x, weight[:, columns], preferred_element_type=jnp.float32
+                ).astype(jnp.bfloat16)
+            d = slices * t + s
+
+            @pl.when(d != c)
+            def _():
+                send(gu_out.at[i, s], gu_in.at[i, c], gu_s.at[i, s], gu_r.at[i, c], {"ctx": d})
+
+    def down(i):
+        source = exp_at(i)
+
+        @pl.when(t == c // slices)
+        def _():
+            total = gu_out[i, lax.rem(c, slices)].astype(jnp.float32)
+            for step in range(1, n_ctx):
+                d = ctx_at(step)
+                arrived(gu_in.at[i, d], gu_s.at[i, 0], gu_r.at[i, d], {"ctx": d})
+                total += gu_in[i, d].astype(jnp.float32)
+            gate, up = total[:, :slice_width], total[:, slice_width:]
+            hidden[i] = (gate * jax.nn.sigmoid(gate) * up).astype(jnp.bfloat16)
+            send(hidden.at[i], hidden.at[i], h_s.at[i], h_r.at[i], core)
+
+        @pl.when(t != c // slices)
+        def _():
+            arrived(hidden.at[i], h_s.at[i], h_r.at[i], core)
+
+        gate_lane = lax.broadcasted_iota(jnp.int32, (chunk, LANES), 1)
+        table = rows[source].reshape(chunk, width + LANES)[:, width:].astype(jnp.float32)
+        mine = (gate_lane == e) | (gate_lane == n_exp + e)
+        scale = jnp.sum(jnp.where(mine, table, 0.0), axis=1, keepdims=True)
+        units = hidden[i]
+        out_width = wd_ref.shape[1]
+        tile = 256 if out_width % 256 == 0 else LANES
+        for at in range(0, out_width, tile):
+            produced = jnp.dot(units, wd_ref[:, at : at + tile], preferred_element_type=jnp.float32)
+            dn_out[i, :, :, at : at + tile] = (
+                (produced * scale).astype(jnp.bfloat16).reshape(n_ctx, tokens, tile)
+            )
+        for step in range(1, n_ctx):
+            d = ctx_at(step)
+            sends.append(
+                send(dn_out.at[i, d], dn_in.at[i, c], dn_s.at[i, step], dn_r.at[i, c], {"ctx": d})
+            )
+
+    def combine(i):
+        for step in range(1, n_ctx):
+            d = ctx_at(step)
+            arrived(dn_in.at[i, d], dn_s.at[i, step], dn_r.at[i, d], {"ctx": d})
+        total = dn_out[i, c].astype(jnp.float32)
+        for step in range(1, n_ctx):
+            total += dn_in[i, ctx_at(step)].astype(jnp.float32)
+        if i == 0:
+            home[...] = total
+        else:
+            z_out[i] = total.astype(jnp.bfloat16)
+            sends.append(
+                send(z_out.at[i], z_in.at[e], zz_s.at[i], zz_r.at[e], {"exp": exp_at(i)})
+            )
+
+    def gather_keys():
+        for step in range(1, n_ctx):
+            d = ctx_at(step)
+            arrived(keys.at[d, t], k_s.at[step], k_r.at[d], {"ctx": d})
+        sends.append(send(keys.at[:, t], keys.at[:, t], kc_s, kc_r, core))
+
+    def mask():
+        own = order_ref[c] * block + lax.broadcasted_iota(jnp.int32, (block, block), 0)
+        at = lax.broadcasted_iota(jnp.int32, (block, block), 1)
+        return jnp.concatenate(
+            [order_ref[d] * block + at <= own for d in range(n_ctx)], axis=1
+        )
+
+    def attend(first, last):
+        visible = mask()
+        key_rows = keys[...].reshape(n_ctx * block, full_width)
+        for h in range(first, last):
+            scores = lax.dot_general(
+                q_ref[:, h * full_width : (h + 1) * full_width], key_rows,
+                (((1,), (1,)), ((), ())), preferred_element_type=jnp.float32,
+            ) * softmax_scale
+            masked = jnp.where(visible, scores, very_negative)
+            top = jnp.max(masked, axis=1, keepdims=True)
+            weights = jnp.where(visible, jnp.exp(masked - top), 0.0)
+            total = jnp.sum(weights, axis=1, keepdims=True)
+            summed = jnp.dot(
+                weights.astype(jnp.bfloat16), key_rows[:, :LATENT],
+                preferred_element_type=jnp.float32,
+            )
+            context_ref[:, h * LATENT : (h + 1) * LATENT] = (summed / total).astype(jnp.bfloat16)
+
+    share_chunk(0)
+    gather_keys()
+    loads[0].wait()
+    loads[1].wait()
+    project(0)
+    loads[2].wait()
+    arrived(keys.at[:, other], kc_s, kc_r, core)
+    cut = [heads * k // 4 for k in range(5)]
+    attend(cut[0], cut[2])
+    loads[3].wait()
+    for i in range(1, n_exp + 2):
+        if i < n_exp:
+            share_chunk(i)
+            if i == 1:
+                attend(cut[2], cut[3])
+            if i == 2:
+                attend(cut[3], cut[4])
+            project(i)
+        if 0 <= i - 1 < n_exp:
+            down(i - 1)
+        if 0 <= i - 2 < n_exp:
+            combine(i - 2)
+
+    result = home[...]
+    for step in range(1, n_exp):
+        d = exp_at(step)
+        arrived(z_in.at[d], zz_s.at[step], zz_r.at[d], {"exp": d})
+        result += z_in[d].astype(jnp.float32)
+    moe_ref[...] = result.astype(moe_ref.dtype)
+
+    for copy in sends:
+        copy.wait_send()
+    for i in range(n_exp):
+        for s in range(slices):
+            d = slices * t + s
+
+            @pl.when(d != c)
+            def _():
+                pltpu.make_async_remote_copy(
+                    src_ref=gu_out.at[i, s], dst_ref=gu_in.at[i, c], send_sem=gu_s.at[i, s],
+                    recv_sem=gu_r.at[i, c], device_id={"ctx": d}, device_id_type=MESH,
+                ).wait_send()
+
+        @pl.when(t == c // slices)
+        def _():
+            pltpu.make_async_remote_copy(
+                src_ref=hidden.at[i], dst_ref=hidden.at[i], send_sem=h_s.at[i],
+                recv_sem=h_r.at[i], device_id=core, device_id_type=MESH,
+            ).wait_send()
+
+
+def fused_body(n_ctx, n_exp, *args):
+    queries, latent_keys, block_order, moe_input, routes, gate_weights, w_gate, w_up, w_down = args
+    wg, wu, wd = w_gate[0], w_up[0], w_down[0]
+    block, q_width = queries.shape
+    heads = q_width // (LATENT + ROPE)
+    tokens = moe_input.shape[0]
+    width, units = wg.shape
+    slice_width, out_width = wd.shape
+    slices = units // slice_width
+    chunk = n_ctx * tokens
+    bf16, f32 = jnp.bfloat16, jnp.float32
+    vmem = pl.BlockSpec(memory_space=pltpu.VMEM)
+    smem = pl.BlockSpec(memory_space=pltpu.SMEM)
+    anywhere = pl.BlockSpec(memory_space=pl.ANY)
+    dma = pltpu.SemaphoreType.DMA
+    by_ctx, by_exp = dma((n_ctx,)), dma((n_exp,))
+    both = dma((n_exp, n_ctx))
+    return pl.pallas_call(
+        functools.partial(kernel, n_ctx, n_exp),
+        out_shape=(
+            jax.ShapeDtypeStruct((block, heads * LATENT), bf16),
+            jax.ShapeDtypeStruct((tokens, out_width), bf16),
+        ),
+        in_specs=[anywhere, vmem, smem, vmem, vmem, vmem, anywhere, anywhere, anywhere],
+        out_specs=(vmem, vmem),
+        scratch_shapes=[
+            pltpu.VMEM(queries.shape, bf16),
+            pltpu.VMEM(wg.shape, bf16),
+            pltpu.VMEM(wu.shape, bf16),
+            pltpu.VMEM(wd.shape, bf16),
+            pltpu.VMEM((n_ctx, 2, tokens // 2, width + LANES), bf16),
+            pltpu.VMEM((n_exp, n_ctx, 2, tokens // 2, width + LANES), bf16),
+            pltpu.VMEM((n_ctx, 2, block // 2, LATENT + ROPE), bf16),
+            pltpu.VMEM((n_exp, slices, chunk, 2 * slice_width), bf16),
+            pltpu.VMEM((n_exp, n_ctx, chunk, 2 * slice_width), bf16),
+            pltpu.VMEM((n_exp, chunk, slice_width), bf16),
+            pltpu.VMEM((n_exp, n_ctx, tokens, out_width), bf16),
+            pltpu.VMEM((n_exp, n_ctx, tokens, out_width), bf16),
+            pltpu.VMEM((n_exp, tokens, out_width), bf16),
+            pltpu.VMEM((n_exp, tokens, out_width), bf16),
+            pltpu.VMEM((tokens, out_width), f32),
+            dma((4,)),
+            by_ctx, by_ctx, by_exp, by_exp, by_exp, by_exp, by_ctx, by_ctx, dma, dma,
+            dma((n_exp, slices)), both, by_exp, by_exp, both, both, by_exp, by_exp,
+        ],
+        compiler_params=pltpu.CompilerParams(
+            collective_id=0, has_side_effects=True, vmem_limit_bytes=48 * 1024 * 1024
+        ),
+    )(queries, latent_keys, block_order, moe_input, routes, gate_weights, wg, wu, wd)
 
 
 def passed_along(block, axis, distance):
@@ -130,4 +436,18 @@
         P("exp", "ctx", "tp"),
     )
     out_specs = (P("ctx", ("exp", "tp")), P(("ctx", "exp"), "tp"))
-    return jax.shard_map(body, mesh=mesh, in_specs=in_specs, out_specs=out_specs, check_vma=False)
+    n_ctx, n_exp, n_tp = mesh.shape["ctx"], mesh.shape["exp"], mesh.shape["tp"]
+
+    def whole(*args):
+        units_slice = args[8].shape[1] // n_ctx
+        width = args[6].shape[1] // n_ctx
+        fits = units_slice % LANES == 0 and width % LANES == 0 and n_ctx * n_exp <= 16 and n_tp == 2
+        inner = functools.partial(fused_body, n_ctx, n_exp) if fits else body
+        return split(inner)(*args)
+
+    def split(inner):
+        return jax.shard_map(
+            inner, mesh=mesh, in_specs=in_specs, out_specs=out_specs, check_vma=False
+        )
+
+    return whole

time: 207 us -> 71.7 us (0.35)
  waiting for transfers between devices: 143 us -> 0 us
  Pallas kernels: 0 us -> 59.6 us
  matrix products: 18.8 us -> 0 us
  between operations: 14.6 us -> 0.65 us
  starting transfers between devices: 13.3 us -> 0 us
  other arithmetic: 2.71 us -> 0 us
  loops' own time: 2.21 us -> 0 us
    all_gather x3 -> x0, waiting for transfers between devices: 112 us -> none  [the longest x1 47.5 us: body(): lax.all_gather(w_up, 'ctx', axis=1, tiled=True)]
    pallas_call x0 -> x1, Pallas kernels: none -> 59.6 us  [fused_body(): pl.pallas_call(functools.partial(kernel, n_ctx, n_exp), out_shape=(jax.Sh...]
    dot_general x11 -> x0, matrix products: 18.8 us -> none  [the longest x4 6.81 us: attend(): jnp.einsum('thc,uc->thu', per_head, key_block, preferred_element_type=jnp...]
    all_to_all x2 -> x0, waiting for transfers between devices: 17.8 us -> none  [the longest x1 17.7 us: body(): lax.all_to_all(outgoing, 'exp', split_axis=0, concat_axis=0, tiled=True)]
    ppermute x3 -> x0, waiting for transfers between devices: 12.2 us -> none  [passed_along(): return lax.ppermute(block, axis, route)]
    all_to_all x2 -> x0, starting transfers between devices: 11 us -> none  [the longest x1 6.45 us: body(): lax.all_to_all(outgoing, 'exp', split_axis=0, concat_axis=0, tiled=True)]
    unnamed x14 -> x17, local copies, waits for them, and re-layouts: 2.5 us -> 10.6 us
    dynamic_slice x4 -> x0, local copies, waits for them, and re-layouts: 2.4 us -> none  [attend(): source_block = block_order[source]]
  transfers between devices with their start and end apart: 8 -> 0, of which waited for: 7 -> 0; matrix products, arithmetic and copies ran while one was open for 12% -> 0% of each run, Pallas kernels for 0% -> 0%
where the time goes in v1:
time: 71.7 us; the launch traced here: 70.9 us
  Pallas kernels  59.6 us (83%)
  local copies, waits for them, and re-layouts  10.6 us (15%)
    pallas_call x1, Pallas kernels, fused_body(): pl.pallas_call(functools.partial(kernel, n_ctx, n_exp), out_shape=(jax.Sh...  59.6 us
    unnamed x17, local copies, waits for them, and re-layouts  10.6 us

profile of v1, /device:TPU:0, one launch (start us, length us, event | category | flops | bytes accessed | tf_op | source)
XLA Modules:
  0.0 70.9 jit_solution(2608086066140967601)
XLA Ops:
  0.6 0.8 %copy.12.routes_ref = s32[32,2]{1,0:T(8,128)S(1)} copy(s32[32,2]{0,1:T(2,128)} %param.13) | data formatting | bytes 512 | tf_op args[4]
  1.4 0.8 %copy.13.gates_ref = f32[32,2]{1,0:T(8,128)S(1)} copy(f32[32,2]{0,1:T(2,128)} %param.14) | data formatting | bytes 512 | tf_op args[5]
  2.1 1.1 %copy.11.k_ref = bf16[128,576]{1,0:T(8,128)(2,1)S(1)} copy(bf16[128,576]{0,1:T(8,128)(2,1)} %param.10) | data formatting | bytes 294912 | tf_op args[1]
  3.2 0.0 copy-start
  3.2 1.3 %copy-done = bf16[128,4608]{1,0:T(8,128)(2,1)S(1)} copy-done((bf16[128,4608]{1,0:T(8,128)(2,1)S(1)}, bf16[128,4608]{1,0:T(8,128)(2,1)}, u32[]{:S(2)}) %copy-start) | copy-done | bytes 1179672
  4.5 0.0 copy-start.1
  4.5 1.2 %copy-done.1 = bf16[1,896,512]{2,1,0:T(8,128)(2,1)S(1)} copy-done((bf16[1,896,512]{2,1,0:T(8,128)(2,1)S(1)}, bf16[1,896,512]{2,1,0:T(8,128)(2,1)}, u32[]{:S(2)}) %copy-start.1) | copy-done | bytes 917528
  5.7 0.0 copy-start.2
  5.7 1.2 %copy-done.2 = bf16[1,896,512]{2,1,0:T(8,128)(2,1)S(1)} copy-done((bf16[1,896,512]{2,1,0:T(8,128)(2,1)S(1)}, bf16[1,896,512]{2,1,0:T(8,128)(2,1)}, u32[]{:S(2)}) %copy-start.2) | copy-done | bytes 917528
  6.8 0.0 copy-start.3
  6.8 1.2 %copy-done.3 = bf16[1,256,1792]{2,1,0:T(8,128)(2,1)S(1)} copy-done((bf16[1,256,1792]{2,1,0:T(8,128)(2,1)S(1)}, bf16[1,256,1792]{2,1,0:T(8,128)(2,1)}, u32[]{:S(2)}) %copy-start.3) | copy-done | bytes 917528
  8.0 0.0 copy-start.4
  8.0 0.9 %copy-done.4 = bf16[32,3584]{1,0:T(8,128)(2,1)S(1)} copy-done((bf16[32,3584]{1,0:T(8,128)(2,1)S(1)}, bf16[32,3584]{1,0:T(8,128)(2,1)}, u32[]{:S(2)}) %copy-start.4) | copy-done | bytes 229400
  9.0 0.0 copy-start.5
  9.0 0.7 copy-done.5
  9.6 59.6 %shard_map.104 = (bf16[128,4096]{1,0:T(8,128)(2,1)S(1)}, bf16[32,1792]{1,0:T(8,128)(2,1)S(1)}) custom-call(bf16[128,4608]{1,0:T(8,128)(2,1)S(1)} %copy-done, bf16[128,576]{1,0:T(8,128)(2,1)S(1)} %copy.11.k_ref, s32[4]{0:T(128)S(1)} %copy-done.5, bf16[32,3584]{1,0:T(8,128)(2,1)S(1)} %copy-done.4, s32[32,2]{1,0:T(8,128)S(1)} %copy.12.routes_ref, ...), custom_call_target="tpu_custom_call" | custom-call | tf_op jit(solution)/shard_map/pallas_call | solution.py:286
  69.2 1.0 %copy.16 = bf16[128,4096]{1,0:T(8,128)(2,1)} copy(bf16[128,4096]{1,0:T(8,128)(2,1)S(1)} %get-tuple-element.4) | data formatting | bytes 2097152
  70.2 0.6 copy.17
Async XLA Ops:
  3.2 1.3 %copy-start = (bf16[128,4608]{1,0:T(8,128)(2,1)S(1)}, bf16[128,4608]{1,0:T(8,128)(2,1)}, u32[]{:S(2)}) copy-start(bf16[128,4608]{1,0:T(8,128)(2,1)} %q_hbm.1) | copy-start | bytes 3538948
  4.5 1.2 %copy-start.1 = (bf16[1,896,512]{2,1,0:T(8,128)(2,1)S(1)}, bf16[1,896,512]{2,1,0:T(8,128)(2,1)}, u32[]{:S(2)}) copy-start(bf16[1,896,512]{2,1,0:T(8,128)(2,1)} %param.15) | copy-start | bytes 2752516
  5.7 1.2 %copy-start.2 = (bf16[1,896,512]{2,1,0:T(8,128)(2,1)S(1)}, bf16[1,896,512]{2,1,0:T(8,128)(2,1)}, u32[]{:S(2)}) copy-start(bf16[1,896,512]{2,1,0:T(8,128)(2,1)} %param.16) | copy-start | bytes 2752516
  6.8 1.2 %copy-start.3 = (bf16[1,256,1792]{2,1,0:T(8,128)(2,1)S(1)}, bf16[1,256,1792]{2,1,0:T(8,128)(2,1)}, u32[]{:S(2)}) copy-start(bf16[1,256,1792]{2,1,0:T(8,128)(2,1)} %param.17) | copy-start | bytes 2752516
  8.0 0.9 %copy-start.4 = (bf16[32,3584]{1,0:T(8,128)(2,1)S(1)}, bf16[32,3584]{1,0:T(8,128)(2,1)}, u32[]{:S(2)}) copy-start(bf16[32,3584]{1,0:T(8,128)(2,1)} %x_ref.1) | copy-start | bytes 688132
  9.0 0.7 copy-start.5

commit v2 on v1

--- a/solution.py
+++ b/solution.py
@@ -18,9 +18,10 @@
 
 def kernel(
     n_ctx, n_exp,
-    q_hbm, k_ref, order_ref, x_ref, routes_ref, gates_ref, wg_hbm, wu_hbm, wd_hbm,
+    q_hbm, k_hbm, order_hbm, x_hbm, routes_hbm, gates_hbm, wg_hbm, wu_hbm, wd_hbm,
     context_ref, moe_ref,
-    q_ref, wg_ref, wu_ref, wd_ref,
+    q_ref, k_ref, order_ref, x_ref, routes_ref, gates_ref, wg_ref, wu_ref, wd_ref,
+    key_columns, values,
     staged, rows, keys, gu_out, gu_in, hidden, dn_out, dn_in, z_out, z_in, home,
     load_sem,
     xs_s, xs_r, xz_s, xz_r, xc_s, xc_r, k_s, k_r, kc_s, kc_r,
@@ -33,7 +34,7 @@
     slices = wg_ref.shape[1] // slice_width
     tokens = x_ref.shape[0]
     half = tokens // 2
-    block = k_ref.shape[0]
+    block = k_ref.shape[1]
     chunk = n_ctx * tokens
     full_width = LATENT + ROPE
     heads = q_ref.shape[1] // full_width
@@ -47,7 +48,11 @@
     loads = [
         pltpu.make_async_copy(src, dst, load_sem.at[i])
         for i, (src, dst) in enumerate(
-            ((wg_hbm, wg_ref), (wu_hbm, wu_ref), (q_hbm, q_ref), (wd_hbm, wd_ref))
+            (
+                (x_hbm, x_ref), (routes_hbm, routes_ref), (gates_hbm, gates_ref),
+                (k_hbm, k_ref), (order_hbm, order_ref), (wg_hbm, wg_ref), (wu_hbm, wu_ref),
+                (q_hbm, q_ref), (wd_hbm, wd_ref),
+            )
         )
     ]
     for load in loads:
@@ -62,9 +67,21 @@
 
     lane = lax.broadcasted_iota(jnp.int32, (tokens, LANES), 1)
     expert_lane = lax.rem(lane, n_exp)
+    square = (tokens, tokens)
+    on_diagonal = lax.broadcasted_iota(jnp.int32, square, 0) == lax.broadcasted_iota(
+        jnp.int32, square, 1
+    )
+    for load in loads[:4]:
+        load.wait()
     dense = jnp.zeros((tokens, LANES), jnp.float32)
-    for j in range(routes_ref.shape[1]):
-        dense += jnp.where(routes_ref[:, j : j + 1] == expert_lane, gates_ref[:, j : j + 1], 0.0)
+    for expert in range(n_exp):
+        line = jnp.sum(
+            jnp.where(routes_ref[...] == expert, gates_ref[...], 0.0), axis=0, keepdims=True
+        )
+        column = jnp.sum(
+            jnp.where(on_diagonal, jnp.broadcast_to(line, square), 0.0), axis=1, keepdims=True
+        )
+        dense += jnp.where(expert_lane == expert, column, 0.0)
     high = dense.astype(jnp.bfloat16).astype(jnp.float32)
     packed = jnp.where(
         lane < n_exp, high, jnp.where(lane < 2 * n_exp, dense - high, 0.0)
@@ -75,7 +92,8 @@
             staged[d, part, :, :width] = x_ref[span, d * width : (d + 1) * width]
             staged[d, part, :, width:] = packed[span, :]
     rows[e, c, t] = staged[c, t]
-    keys[c, t] = k_ref[pl.ds(pl.multiple_of(t * (block // 2), block // 2), block // 2), :]
+    part_width = full_width // 2
+    keys[c, t] = k_ref[pl.ds(pl.multiple_of(t * part_width, part_width), part_width), :]
 
     pl.semaphore_wait(barrier, n_ctx + n_exp - 1)
 
@@ -199,44 +217,45 @@
 
     def attend(first, last):
         visible = mask()
-        key_rows = keys[...].reshape(n_ctx * block, full_width)
         for h in range(first, last):
-            scores = lax.dot_general(
-                q_ref[:, h * full_width : (h + 1) * full_width], key_rows,
-                (((1,), (1,)), ((), ())), preferred_element_type=jnp.float32,
+            scores = jnp.dot(
+                q_ref[:, h * full_width : (h + 1) * full_width], key_columns[...],
+                preferred_element_type=jnp.float32,
             ) * softmax_scale
             masked = jnp.where(visible, scores, very_negative)
             top = jnp.max(masked, axis=1, keepdims=True)
             weights = jnp.where(visible, jnp.exp(masked - top), 0.0)
             total = jnp.sum(weights, axis=1, keepdims=True)
             summed = jnp.dot(
-                weights.astype(jnp.bfloat16), key_rows[:, :LATENT],
-                preferred_element_type=jnp.float32,
+                weights.astype(jnp.bfloat16), values[...], preferred_element_type=jnp.float32
             )
             context_ref[:, h * LATENT : (h + 1) * LATENT] = (summed / total).astype(jnp.bfloat16)
 
     share_chunk(0)
     gather_keys()
-    loads[0].wait()
-    loads[1].wait()
+    loads[5].wait()
+    loads[6].wait()
     project(0)
-    loads[2].wait()
+    loads[4].wait()
+    loads[7].wait()
     arrived(keys.at[:, other], kc_s, kc_r, core)
+    for d in range(n_ctx):
+        block_keys = keys[d].reshape(full_width, block)
+        key_columns[:, d * block : (d + 1) * block] = block_keys
+        values[d * block : (d + 1) * block, :] = block_keys[:LATENT, :].T
     cut = [heads * k // 4 for k in range(5)]
     attend(cut[0], cut[2])
-    loads[3].wait()
-    for i in range(1, n_exp + 2):
-        if i < n_exp:
-            share_chunk(i)
-            if i == 1:
-                attend(cut[2], cut[3])
-            if i == 2:
-                attend(cut[3], cut[4])
-            project(i)
-        if 0 <= i - 1 < n_exp:
-            down(i - 1)
-        if 0 <= i - 2 < n_exp:
-            combine(i - 2)
+    loads[8].wait()
+    down(0)
+    for i in range(1, n_exp):
+        share_chunk(i)
+        if i <= 2:
+            attend(cut[i + 1], cut[i + 2])
+        project(i)
+    for i in range(1, n_exp):
+        down(i)
+        combine(i - 1)
+    combine(n_exp - 1)
 
     result = home[...]
     for step in range(1, n_exp):
@@ -278,8 +297,7 @@
     chunk = n_ctx * tokens
     bf16, f32 = jnp.bfloat16, jnp.float32
     vmem = pl.BlockSpec(memory_space=pltpu.VMEM)
-    smem = pl.BlockSpec(memory_space=pltpu.SMEM)
-    anywhere = pl.BlockSpec(memory_space=pl.ANY)
+    hbm = pl.BlockSpec(memory_space=pltpu.HBM)
     dma = pltpu.SemaphoreType.DMA
     by_ctx, by_exp = dma((n_ctx,)), dma((n_exp,))
     both = dma((n_exp, n_ctx))
@@ -289,16 +307,23 @@
             jax.ShapeDtypeStruct((block, heads * LATENT), bf16),
             jax.ShapeDtypeStruct((tokens, out_width), bf16),
         ),
-        in_specs=[anywhere, vmem, smem, vmem, vmem, vmem, anywhere, anywhere, anywhere],
+        in_specs=[hbm] * 9,
         out_specs=(vmem, vmem),
         scratch_shapes=[
             pltpu.VMEM(queries.shape, bf16),
+            pltpu.VMEM((LATENT + ROPE, block), bf16),
+            pltpu.SMEM(block_order.shape, jnp.int32),
+            pltpu.VMEM(moe_input.shape, bf16),
+            pltpu.VMEM(routes.shape[::-1], jnp.int32),
+            pltpu.VMEM(gate_weights.shape[::-1], f32),
             pltpu.VMEM(wg.shape, bf16),
             pltpu.VMEM(wu.shape, bf16),
             pltpu.VMEM(wd.shape, bf16),
+            pltpu.VMEM((LATENT + ROPE, n_ctx * block), bf16),
+            pltpu.VMEM((n_ctx * block, LATENT), bf16),
             pltpu.VMEM((n_ctx, 2, tokens // 2, width + LANES), bf16),
             pltpu.VMEM((n_exp, n_ctx, 2, tokens // 2, width + LANES), bf16),
-            pltpu.VMEM((n_ctx, 2, block // 2, LATENT + ROPE), bf16),
+            pltpu.VMEM((n_ctx, 2, (LATENT + ROPE) // 2, block), bf16),
             pltpu.VMEM((n_exp, slices, chunk, 2 * slice_width), bf16),
             pltpu.VMEM((n_exp, n_ctx, chunk, 2 * slice_width), bf16),
             pltpu.VMEM((n_exp, chunk, slice_width), bf16),
@@ -307,14 +332,16 @@
             pltpu.VMEM((n_exp, tokens, out_width), bf16),
             pltpu.VMEM((n_exp, tokens, out_width), bf16),
             pltpu.VMEM((tokens, out_width), f32),
-            dma((4,)),
+            dma((9,)),
             by_ctx, by_ctx, by_exp, by_exp, by_exp, by_exp, by_ctx, by_ctx, dma, dma,
             dma((n_exp, slices)), both, by_exp, by_exp, both, both, by_exp, by_exp,
         ],
         compiler_params=pltpu.CompilerParams(
-            collective_id=0, has_side_effects=True, vmem_limit_bytes=48 * 1024 * 1024
+            collective_id=0, has_side_effects=True, vmem_limit_bytes=64 * 1024 * 1024
         ),
-    )(queries, latent_keys, block_order, moe_input, routes, gate_weights, wg, wu, wd)
+    )(
+        queries, latent_keys.T, block_order, moe_input, routes.T, gate_weights.T, wg, wu, wd
+    )
 
 
 def passed_along(block, axis, distance):
@@ -441,7 +468,7 @@
     def whole(*args):
         units_slice = args[8].shape[1] // n_ctx
         width = args[6].shape[1] // n_ctx
-        fits = units_slice % LANES == 0 and width % LANES == 0 and n_ctx * n_exp <= 16 and n_tp == 2
+        fits = units_slice % LANES == 0 and width % LANES == 0 and n_ctx * n_exp <= 16 and n_exp > 2 and n_tp == 2
         inner = functools.partial(fused_body, n_ctx, n_exp) if fits else body
         return split(inner)(*args)
 

time: 71.7 us -> 59.6 us (0.83)
  local copies, waits for them, and re-layouts: 10.6 us -> 2.97 us
  Pallas kernels: 59.6 us -> 55.8 us
    unnamed x17 -> x4, local copies, waits for them, and re-layouts: 10.6 us -> 2.97 us
    pallas_call x1, Pallas kernels: 59.6 us -> 55.8 us  [fused_body(): pl.pallas_call(functools.partial(kernel, n_ctx, n_exp), out_shape=(jax.Sh...]
where the time goes in v2:
time: 59.6 us; the launch traced here: 59.4 us
  Pallas kernels  55.8 us (94%)
  local copies, waits for them, and re-layouts  2.97 us (5%)
  between operations  0.65 us (1%)
    pallas_call x1, Pallas kernels, fused_body(): pl.pallas_call(functools.partial(kernel, n_ctx, n_exp), out_shape=(jax.Sh...  55.8 us
    unnamed x4, local copies, waits for them, and re-layouts  2.97 us

profile of v2, /device:TPU:0, one launch (start us, length us, event | category | flops | bytes accessed | tf_op | source)
XLA Modules:
  0.0 59.4 jit_solution(1426846294315582129)
XLA Ops:
  0.6 55.8 %shard_map.104 = (bf16[128,4096]{1,0:T(8,128)(2,1)}, bf16[32,1792]{1,0:T(8,128)(2,1)}) custom-call(bf16[128,4608]{1,0:T(8,128)(2,1)} %q_hbm.1, bf16[576,128]{1,0:T(8,128)(2,1)} %bitcast.9, s32[4]{0:T(128)} %order_hbm.1, bf16[32,3584]{1,0:T(8,128)(2,1)} %x_hbm.1, s32[2,32]{1,0:T(2,128)} %bitcast.10, f32[2,32]{1,0:T(2,128)} %bitcast.11, ...), custom_call_target="tpu_custom_call" | custom-call | tf_op jit(solution)/shard_map/pallas_call | solution.py:304
  56.5 0.0 copy-start
  56.5 2.3 %copy.13 = bf16[128,4096]{1,0:T(8,128)(2,1)} copy(bf16[128,4096]{1,0:T(8,128)(2,1)} %get-tuple-element.4) | data formatting | bytes 2097152
  58.8 0.0 copy-done
  58.8 0.6 %copy.14 = bf16[32,1792]{1,0:T(8,128)(2,1)} copy(bf16[32,1792]{1,0:T(8,128)(2,1)S(1)} %copy-done) | data formatting | bytes 229376
Async XLA Ops:
  56.5 2.3 %copy-start = (bf16[32,1792]{1,0:T(8,128)(2,1)S(1)}, bf16[32,1792]{1,0:T(8,128)(2,1)}, u32[]{:S(2)}) copy-start(bf16[32,1792]{1,0:T(8,128)(2,1)} %get-tuple-element.5) | copy-start | bytes 344068
